TPU v7x, 32 devices: a whole 2x2x4 slice. The times are simulated.
32 devices in a mesh: freq: 16 (over z, y, x), panel: 2 (over core).
Axes of the slice: x: 2, y: 2, z: 4, core: 2. Of those that a mesh axis runs over, the one named last changes fastest.
Arguments:
- shot_gathers: bfloat16 [64, 2048, 2048], P('freq', 'panel'), may hold values from -6 to 6
- aperture_blocks: int32 [32], replicated, may hold values from 8 to 16, as said below
- taper_index: int32 [32], replicated, may hold values from 0 to 3
Outputs:
- predicted: bfloat16 [64, 2048, 128], P('freq', 'panel')
Inputs may be any that keep to these rules, and one draw needn't show every extreme that they name: `aperture_blocks`: aperture of each frequency in blocks of 128 surface points, counted from the first point; the largest value occurs in every draw.
All inputs are finite; a program needn't handle non-finite values.
Results may differ from a plain program's by a relative error of at most 0.0076.
Values may be sent and summed in bfloat16 or wider, within the bound.
A program may use at most 128 MiB of HBM per device.

v0:
```python
import math
import jax
import jax.numpy as jnp
from jax import lax
from jax.sharding import PartitionSpec as P

SW = 128
BLOCK = 128
F_DEV = 2
TAPER = 64


def transform_tables(freq_total, time_total):
    bins = jnp.arange(freq_total, dtype=jnp.int32) + 1
    times = jnp.arange(time_total, dtype=jnp.int32)
    phase = bins[:, None] * times[None, :] % time_total
    angle = phase.astype(jnp.float32) * (2.0 * math.pi / time_total)
    scale = 1.0 / math.sqrt(time_total)
    forward = jnp.stack([jnp.cos(angle) * scale, -jnp.sin(angle) * scale], axis=1).astype(
        jnp.bfloat16
    )
    inverse = jnp.stack([jnp.cos(angle), -jnp.sin(angle)], axis=1).astype(jnp.bfloat16)
    return (forward, inverse)


def taper_weights(aperture, taper_level, surface_points):
    ends = aperture * BLOCK
    ramp = jnp.minimum(TAPER * (1 + taper_level), ends)
    begins = ends - ramp
    offset = (surface_points - begins + 1).astype(jnp.float32)
    wave = jnp.cos(0.5 * math.pi * offset / (ramp + 1).astype(jnp.float32))
    inside = jnp.where(surface_points < ends, wave * wave, jnp.zeros_like(wave))
    return jnp.where(surface_points < begins, jnp.ones_like(wave), inside)


def body(shot_gathers, aperture_blocks, taper_index):
    time_local, rows_local, points_total = shot_gathers.shape
    owners = lax.axis_size("freq")
    slot_count = 2 * F_DEV
    time_total = time_local * owners
    freq_total = F_DEV * owners
    owner_index = lax.axis_index("freq")
    panel_index = lax.axis_index("panel")
    owner_range = jnp.arange(owners, dtype=jnp.int32)
    freq_range = jnp.arange(freq_total, dtype=jnp.int32)
    assignment = freq_range.reshape(owners, F_DEV)
    forward, inverse = transform_tables(freq_total, time_total)
    selector = (assignment.reshape(-1)[:, None] == freq_range[None, :]).astype(jnp.bfloat16)
    picked_forward = jnp.dot(
        selector, forward.reshape(freq_total, 2 * time_total), preferred_element_type=jnp.float32
    ).astype(jnp.bfloat16)
    forward_rows = (
        picked_forward.reshape(owners, F_DEV, 2, time_total)
        .transpose(1, 2, 0, 3)
        .reshape(slot_count, owners, time_total)
    )
    picked_inverse = jnp.dot(
        selector, inverse.reshape(freq_total, 2 * time_total), preferred_element_type=jnp.float32
    ).astype(jnp.bfloat16)
    inverse_rows = picked_inverse.reshape(owners * slot_count, owners, time_local)
    trace_width = rows_local * points_total // owners
    outgoing_time = shot_gathers.reshape(time_local, owners, trace_width)
    series = lax.all_to_all(outgoing_time, "freq", split_axis=1, concat_axis=0, tiled=True)[:, 0, :]
    spectra = jnp.einsum(
        "qot,tw->qow", forward_rows, series, preferred_element_type=jnp.float32
    ).astype(jnp.bfloat16)
    own_spectra = lax.all_to_all(spectra, "freq", split_axis=1, concat_axis=1, tiled=True)
    own_spectra = own_spectra.reshape(F_DEV, 2, rows_local, points_total)
    mine = owner_range[:, None] == owner_index
    my_freqs = jnp.sum(jnp.where(mine, assignment, jnp.zeros_like(assignment)), axis=0)
    matches = my_freqs[:, None] == freq_range[None, :]
    my_aperture = jnp.sum(jnp.where(matches, aperture_blocks[None, :], 0), axis=1)
    my_taper = jnp.sum(jnp.where(matches, taper_index[None, :], 0), axis=1)
    local_points = panel_index * rows_local + jnp.arange(rows_local, dtype=jnp.int32)
    weights = taper_weights(my_aperture[:, None], my_taper[:, None], local_points[None, :])
    tapered = (weights[:, None, :, None] * own_spectra[:, :, :, :SW].astype(jnp.float32)).astype(
        jnp.bfloat16
    )
    piece = lax.all_gather(tapered, "panel", axis=2, tiled=True)
    updated_list = []
    for slot_index in range(F_DEV):
        left_block = own_spectra[slot_index]
        stacked_left = jnp.concatenate([left_block[0], left_block[1]], axis=1)
        real_side = jnp.concatenate([piece[slot_index, 0], -piece[slot_index, 1]], axis=0)
        imag_side = jnp.concatenate([piece[slot_index, 1], piece[slot_index, 0]], axis=0)
        stacked_right = jnp.stack([real_side, imag_side], axis=0)
        updated = jnp.einsum(
            "rk,cks->crs", stacked_left, stacked_right, preferred_element_type=jnp.float32
        )
        updated_list.append(updated)
    summed = jnp.stack(updated_list, axis=0)
    multiples = (summed * (-1.0 / math.sqrt(points_total))).astype(jnp.bfloat16)
    output_width = rows_local * SW // owners
    outgoing_freq = multiples.reshape(slot_count, owners, output_width)
    output_scale = 1.0 / math.sqrt(freq_total)
    values = lax.all_to_all(outgoing_freq, "freq", split_axis=1, concat_axis=0, tiled=True)[:, 0, :]
    traces = (
        jnp.einsum("qgt,qw->tgw", inverse_rows, values, preferred_element_type=jnp.float32)
        * output_scale
    )
    result = lax.all_to_all(
        traces.astype(jnp.bfloat16), "freq", split_axis=1, concat_axis=1, tiled=True
    )
    return result.reshape(time_local, rows_local, SW)


def solution(mesh):
    return jax.shard_map(
        body,
        mesh=mesh,
        in_specs=(P("freq", "panel", None), P(), P()),
        out_specs=P("freq", "panel", None),
        check_vma=False,
    )
```

profile of v0, /device:TPU:0, one launch (start us, length us, event | category | flops | bytes accessed | tf_op | source)
XLA Modules:
  0.0 1098.2 jit_solution(10738489167989122141)
XLA Ops:
  6.5 17.0 %reshape.339 = bf16[4,16,131072]{2,1,0:T(8,128)(2,1)} reshape(bf16[4,1024,2048]{2,1,0:T(8,128)(2,1)} %param.3) | data formatting | bytes 33554432 | tf_op jit(solution)/shard_map/reshape | solution.py:62
  23.5 22.1 %copy.53 = bf16[4,16,131072]{2,0,1:T(4,128)(2,1)} copy(bf16[4,16,131072]{2,1,0:T(8,128)(2,1)} %reshape.339) | data formatting | bytes 33554432 | tf_op jit(solution)/shard_map/reshape | solution.py:62
  45.6 8.4 all-to-all-start
  54.0 0.2 fusion.29
  54.3 0.1 convolution_convert_fusion.2
  54.5 314.8 %all-to-all-done = bf16[4,16,131072]{2,0,1:T(4,128)(2,1)} async-done(((bf16[4,16,131072]{2,0,1:T(4,128)(2,1)}), bf16[4,16,131072]{2,0,1:T(4,128)(2,1)}, u32[]{:S(2)}, u32[]{:S(2)}) %all-to-all-start) | async-done | bytes 16777248 | tf_op jit(solution)/shard_map/all_to_all | solution.py:63
  369.3 15.0 %reshape.343 = bf16[64,131072,1]{1,0,2:T(8,128)(2,1)} reshape(bf16[16,4,1,131072]{3,1,0,2:T(4,128)(2,1)} %bitcast.3) | data formatting | bytes 33554432 | tf_op jit(solution)/shard_map/squeeze | solution.py:63
  384.4 11.4 %convolution_convert_fusion = bf16[4,16,131072]{2,1,0:T(8,128)(2,1)} fusion(bf16[4,16,64]{2,1,0:T(8,128)(2,1)S(1)} %bitcast.61, bf16[64,131072,1]{1,0,2:T(8,128)(2,1)} %reshape.343), kind=kOutput, calls=%fused_computation | convolution fusion | flops 1082130432 | bytes 33562624 | tf_op jit(solution)/shard_map/qot,tw->qow/dot_general | solution.py:64
  395.8 22.1 %copy.54 = bf16[4,16,131072]{2,0,1:T(4,128)(2,1)} copy(bf16[4,16,131072]{2,1,0:T(8,128)(2,1)} %convolution_convert_fusion) | data formatting | bytes 33554432 | tf_op jit(solution)/shard_map/convert_element_type | solution.py:66
  417.9 73.2 %all-to-all-start.1 = ((bf16[4,16,131072]{2,0,1:T(4,128)(2,1)}), bf16[4,16,131072]{2,0,1:T(4,128)(2,1)}, u32[]{:S(2)}, u32[]{:S(2)}) async-start(bf16[4,16,131072]{2,0,1:T(4,128)(2,1)} %copy.54), calls=%async_computation.1 | async-start | bytes 33554432 | tf_op jit(solution)/shard_map/all_to_all | solution.py:67
  491.1 0.2 all-gather.2.cloned.1.call-start
  491.5 0.2 select_reduce_fusion.1
  491.7 0.2 compare_select_fusion.1
  491.9 311.9 %all-to-all-done.1 = bf16[4,16,131072]{2,0,1:T(4,128)(2,1)} async-done(((bf16[4,16,131072]{2,0,1:T(4,128)(2,1)}), bf16[4,16,131072]{2,0,1:T(4,128)(2,1)}, u32[]{:S(2)}, u32[]{:S(2)}) %all-to-all-start.1) | async-done | bytes 16777248 | tf_op jit(solution)/shard_map/all_to_all | solution.py:67
  803.8 18.5 %copy.55 = bf16[4,16,131072]{2,1,0:T(8,128)(2,1)} copy(bf16[4,16,131072]{2,0,1:T(4,128)(2,1)} %all-to-all-done.1) | data formatting | bytes 33554432 | tf_op jit(solution)/shard_map/all_to_all | solution.py:67
  822.3 17.0 %reshape.340 = bf16[2,2,1024,2048]{3,2,1,0:T(8,128)(2,1)} reshape(bf16[4,16,131072]{2,1,0:T(8,128)(2,1)} %copy.55) | data formatting | bytes 33554432 | tf_op jit(solution)/shard_map/reshape | solution.py:68
  839.3 1.3 slice.52
  840.6 0.5 copy.63
  841.2 1.2 multiply_convert_fusion
  842.4 86.1 %slice_reduce_fusion.3 = (bf16[16,131072]{1,0:T(8,128)(2,1)}, bf16[16,131072]{1,0:T(8,128)(2,1)}, bf16[16,131072]{1,0:T(8,128)(2,1)}, bf16[16,131072]{1,0:T(8,128)(2,1)}) fusion(bf16[4,16,131072]{2,0,1:T(4,128)(2,1)} %all-to-all-done.1), kind=kLoop, calls=%fused_computation.7 | loop fusion | bytes 33554432 | tf_op jit(solution)/shard_map/slice | solution.py:83
  928.5 4.8 squeeze.44
  933.3 4.8 squeeze.43
  938.1 4.8 squeeze.40
  942.9 4.8 squeeze.39
  947.8 1.3 fusion.33
  949.0 1.8 slice_bitcast_fusion.2
  950.9 0.2 maximum_bitcast_fusion.10
  951.1 0.2 maximum_bitcast_fusion.8
  951.3 0.5 copy-done.3
  951.8 1.5 copy-done.1
  953.4 2.4 fusion.15
  955.7 1.1 copy-done.2
  956.8 2.4 fusion.18
  959.2 0.3 fusion.14
  959.5 0.7 copy.57
  960.1 0.8 convert_element_type.91
  960.9 1.8 copy.58
  962.7 72.7 %all-to-all-start.2 = ((bf16[4,16,8192]{2,0,1:T(4,128)(2,1)}), bf16[4,16,8192]{2,0,1:T(4,128)(2,1)S(1)}, u32[]{:S(2)}, u32[]{:S(2)}) async-start(bf16[4,16,8192]{2,0,1:T(4,128)(2,1)} %copy.58), calls=%async_computation.2 | async-start | bytes 2097152 | tf_op jit(solution)/shard_map/all_to_all | solution.py:96
  1035.5 0.1 convolution_convert_fusion.1
  1035.6 0.6 reshape.341
  1036.2 0.3 copy.60
  1036.5 21.5 %all-to-all-done.2 = bf16[4,16,8192]{2,0,1:T(4,128)(2,1)S(1)} async-done(((bf16[4,16,8192]{2,0,1:T(4,128)(2,1)}), bf16[4,16,8192]{2,0,1:T(4,128)(2,1)S(1)}, u32[]{:S(2)}, u32[]{:S(2)}) %all-to-all-start.2) | async-done | bytes 1048608 | tf_op jit(solution)/shard_map/all_to_all | solution.py:96
  1057.9 0.3 reshape.346
  1058.2 0.4 fusion.1
  1058.6 0.8 copy.61
  1059.5 30.0 %all_to_all.40 = bf16[4,16,8192]{2,0,1:T(4,128)(2,1)S(1)} all-to-all(bf16[4,16,8192]{2,0,1:T(4,128)(2,1)S(1)} %copy.61), channel_id=1, replica_groups=mesh['freq'=16,'panel'=2] {'freq'}, dimensions={1} | all-to-all | bytes 2097152 | tf_op jit(solution)/shard_map/all_to_all | solution.py:101
  1089.5 0.6 copy.62
  1090.1 1.3 reshape.342
  (23 shorter events, 0.5 us)
Async XLA Ops:
  45.6 323.7 %all-to-all-start = ((bf16[4,16,131072]{2,0,1:T(4,128)(2,1)}), bf16[4,16,131072]{2,0,1:T(4,128)(2,1)}, u32[]{:S(2)}, u32[]{:S(2)}) async-start(bf16[4,16,131072]{2,0,1:T(4,128)(2,1)} %copy.53), calls=%async_computation | async-start | bytes 33554432 | tf_op jit(solution)/shard_map/all_to_all | solution.py:63
  417.9 73.6 %copy-start.4 = (s32[32]{0:T(128)S(1)}, s32[32]{0:T(128)}, u32[]{:S(2)}) copy-start(s32[32]{0:T(128)} %param.4) | copy-start | bytes 388
  417.9 73.6 %copy-start.5 = (s32[32]{0:T(128)S(1)}, s32[32]{0:T(128)}, u32[]{:S(2)}) copy-start(s32[32]{0:T(128)} %param.5) | copy-start | bytes 388
  417.9 385.9 %all-to-all-start.1 = ((bf16[4,16,131072]{2,0,1:T(4,128)(2,1)}), bf16[4,16,131072]{2,0,1:T(4,128)(2,1)}, u32[]{:S(2)}, u32[]{:S(2)}) async-start(bf16[4,16,131072]{2,0,1:T(4,128)(2,1)} %copy.54), calls=%async_computation.1 | async-start | bytes 33554432 | tf_op jit(solution)/shard_map/all_to_all | solution.py:67
  491.1 456.6 %all-gather.2.cloned.1.call-start = ((), (), s32[]{:S(2)}) async-start(), calls=%async_computation.4 | async-start | bytes 3145728 | tf_op jit(solution)/shard_map/all_gather | solution.py:79
  949.0 2.8 copy-start.3
  950.8 2.5 copy-start.1
  953.4 2.4 copy-start
  953.4 3.5 copy-start.2
  962.7 95.3 %all-to-all-start.2 = ((bf16[4,16,8192]{2,0,1:T(4,128)(2,1)}), bf16[4,16,8192]{2,0,1:T(4,128)(2,1)S(1)}, u32[]{:S(2)}, u32[]{:S(2)}) async-start(bf16[4,16,8192]{2,0,1:T(4,128)(2,1)} %copy.58), calls=%async_computation.2 | async-start | bytes 2097152 | tf_op jit(solution)/shard_map/all_to_all | solution.py:96
Sparse Core Ops, SparseCore 0:
  842.5 77.6 all-gather.1
where the time goes:
time: 1100 us
  waiting for transfers between devices  648 us (59%)
  local copies, waits for them, and re-layouts  231 us (21%)
  starting transfers between devices  154 us (14%)
  blocking collectives  30 us (3%)
  matrix products  16.8 us (2%)
  between operations  13.6 us (1%)
    all_to_all x1, waiting for transfers between devices, body(): lax.all_to_all(outgoing_time, 'freq', split_axis=1, concat_axis=0, tiled=...  315 us
    all_to_all x1, waiting for transfers between devices, body(): lax.all_to_all(spectra, 'freq', split_axis=1, concat_axis=1, tiled=True)  312 us
    slice x1, local copies, waits for them, and re-layouts, body(): stacked_left = jnp.concatenate([left_block[0], left_block[1]], axis=1)  86.1 us
    all_to_all x1, starting transfers between devices, body(): lax.all_to_all(spectra, 'freq', split_axis=1, concat_axis=1, tiled=True)  73.2 us
    all_to_all x1, starting transfers between devices, body(): lax.all_to_all(outgoing_freq, 'freq', split_axis=1, concat_axis=0, tiled=...  72.7 us
    reshape x2, local copies, waits for them, and re-layouts, body(): outgoing_time = shot_gathers.reshape(time_local, owners, trace_width)  39.1 us
    all_to_all x1, blocking collectives, body(): lax.all_to_all(traces.astype(jnp.bfloat16), 'freq', split_axis=1, concat_...  30 us
    convert_element_type x1, local copies, waits for them, and re-layouts, body(): spectra = jnp.einsum('qot,tw->qow', forward_rows, series, preferred_eleme...  22.1 us
  transfers between devices with their start and end apart: 4, of which 3 were waited for; matrix products, arithmetic and copies ran while one was open for 10% of the time, Pallas kernels for 0%

commit v1 on v0

--- a/solution.py
+++ b/solution.py
@@ -98,9 +98,19 @@
         jnp.einsum("qgt,qw->tgw", inverse_rows, values, preferred_element_type=jnp.float32)
         * output_scale
     )
-    result = lax.all_to_all(
-        traces.astype(jnp.bfloat16), "freq", split_axis=1, concat_axis=1, tiled=True
-    )
+    value = traces.astype(jnp.bfloat16)
+    ways, here = (lax.axis_size("freq"), lax.axis_index("freq"))
+    width = value.shape[1] // ways
+    dims = list(value.shape)
+    dims[1] = width
+    height = dims[1]
+    dims[1] = height * ways
+    result = jnp.zeros(dims, value.dtype)
+    for mask in range(ways):
+        part = lax.dynamic_slice_in_dim(value, (here ^ mask) * width, width, axis=1)
+        if mask:
+            part = lax.ppermute(part, "freq", [(d, d ^ mask) for d in range(ways)])
+        result = lax.dynamic_update_slice_in_dim(result, part, (here ^ mask) * height, axis=1)
     return result.reshape(time_local, rows_local, SW)
 
 

time: 1100 us -> 1160 us (1.055)
  local copies, waits for them, and re-layouts: 231 us -> 268 us
  blocking collectives: 30 us -> 0 us
  starting transfers between devices: 154 us -> 181 us
  waiting for transfers between devices: 648 us -> 668 us
    dynamic_update_slice x0 -> x16, local copies, waits for them, and re-layouts: none -> 34 us  [body(): lax.dynamic_update_slice_in_dim(result, part, (here ^ mask) * height, axi...]
    all_to_all x1 -> x0, blocking collectives: 30 us -> none  [body(): lax.all_to_all(traces.astype(jnp.bfloat16), 'freq', split_axis=1, concat_...]
    ppermute x0 -> x15, starting transfers between devices: none -> 25.9 us  [body(): part = lax.ppermute(part, 'freq', [(d, d ^ mask) for d in range(ways)])]
    ppermute x0 -> x15, waiting for transfers between devices: none -> 20.4 us  [body(): part = lax.ppermute(part, 'freq', [(d, d ^ mask) for d in range(ways)])]
  transfers between devices with their start and end apart: 4 -> 19, of which waited for: 3 -> 8; matrix products, arithmetic and copies ran while one was open for 10% -> 12% of each run, Pallas kernels for 0% -> 0%
where the time goes in v1:
time: 1160 us; the launch traced here: 1150 us
  waiting for transfers between devices  668 us (58%)
  local copies, waits for them, and re-layouts  268 us (23%)
  starting transfers between devices  181 us (16%)
  matrix products  16.8 us (1%)
  between operations  14.2 us (1%)
    all_to_all x1, waiting for transfers between devices, body(): lax.all_to_all(outgoing_time, 'freq', split_axis=1, concat_axis=0, tiled=...  315 us
    all_to_all x1, waiting for transfers between devices, body(): lax.all_to_all(spectra, 'freq', split_axis=1, concat_axis=1, tiled=True)  312 us
    slice x1, local copies, waits for them, and re-layouts, body(): stacked_left = jnp.concatenate([left_block[0], left_block[1]], axis=1)  86 us
    all_to_all x1, starting transfers between devices, body(): lax.all_to_all(spectra, 'freq', split_axis=1, concat_axis=1, tiled=True)  73.2 us
    all_to_all x1, starting transfers between devices, body(): lax.all_to_all(outgoing_freq, 'freq', split_axis=1, concat_axis=0, tiled=...  72.7 us
    reshape x2, local copies, waits for them, and re-layouts, body(): outgoing_time = shot_gathers.reshape(time_local, owners, trace_width)  39.1 us
    dynamic_update_slice x16, local copies, waits for them, and re-layouts, body(): lax.dynamic_update_slice_in_dim(result, part, (here ^ mask) * height, axi...  34 us
    ppermute x15, starting transfers between devices, body(): part = lax.ppermute(part, 'freq', [(d, d ^ mask) for d in range(ways)])  25.9 us
  transfers between devices with their start and end apart: 19, of which 8 were waited for; matrix products, arithmetic and copies ran while one was open for 12% of the time, Pallas kernels for 0%

profile of v1, /device:TPU:0, one launch (start us, length us, event | category | flops | bytes accessed | tf_op | source)
XLA Modules:
  0.0 1150.7 jit_solution(17960798767083741591)
XLA Ops:
  6.5 17.0 %reshape.339 = bf16[4,16,131072]{2,1,0:T(8,128)(2,1)} reshape(bf16[4,1024,2048]{2,1,0:T(8,128)(2,1)} %param.3) | data formatting | bytes 33554432 | tf_op jit(solution)/shard_map/reshape | solution.py:62
  23.5 22.2 %copy.46 = bf16[4,16,131072]{2,0,1:T(4,128)(2,1)} copy(bf16[4,16,131072]{2,1,0:T(8,128)(2,1)} %reshape.339) | data formatting | bytes 33554432 | tf_op jit(solution)/shard_map/reshape | solution.py:62
  45.7 8.4 all-to-all-start
  54.6 314.8 %all-to-all-done = bf16[4,16,131072]{2,0,1:T(4,128)(2,1)} async-done(((bf16[4,16,131072]{2,0,1:T(4,128)(2,1)}), bf16[4,16,131072]{2,0,1:T(4,128)(2,1)}, u32[]{:S(2)}, u32[]{:S(2)}) %all-to-all-start) | async-done | bytes 16777248 | tf_op jit(solution)/shard_map/all_to_all | solution.py:63
  369.4 15.0 %reshape.343 = bf16[64,131072,1]{1,0,2:T(8,128)(2,1)} reshape(bf16[16,4,1,131072]{3,1,0,2:T(4,128)(2,1)} %bitcast.3) | data formatting | bytes 33554432 | tf_op jit(solution)/shard_map/squeeze | solution.py:63
  384.4 11.4 convolution_convert_fusion
  395.9 22.2 %copy.47 = bf16[4,16,131072]{2,0,1:T(4,128)(2,1)} copy(bf16[4,16,131072]{2,1,0:T(8,128)(2,1)} %convolution_convert_fusion) | data formatting | bytes 33554432 | tf_op jit(solution)/shard_map/convert_element_type | solution.py:66
  418.0 73.2 %all-to-all-start.1 = ((bf16[4,16,131072]{2,0,1:T(4,128)(2,1)}), bf16[4,16,131072]{2,0,1:T(4,128)(2,1)}, u32[]{:S(2)}, u32[]{:S(2)}) async-start(bf16[4,16,131072]{2,0,1:T(4,128)(2,1)} %copy.47), calls=%async_computation.1 | async-start | bytes 33554432 | tf_op jit(solution)/shard_map/all_to_all | solution.py:67
  492.3 311.6 %all-to-all-done.1 = bf16[4,16,131072]{2,0,1:T(4,128)(2,1)} async-done(((bf16[4,16,131072]{2,0,1:T(4,128)(2,1)}), bf16[4,16,131072]{2,0,1:T(4,128)(2,1)}, u32[]{:S(2)}, u32[]{:S(2)}) %all-to-all-start.1) | async-done | bytes 16777248 | tf_op jit(solution)/shard_map/all_to_all | solution.py:67
  804.0 18.6 %copy.48 = bf16[4,16,131072]{2,1,0:T(8,128)(2,1)} copy(bf16[4,16,131072]{2,0,1:T(4,128)(2,1)} %all-to-all-done.1) | data formatting | bytes 33554432 | tf_op jit(solution)/shard_map/all_to_all | solution.py:67
  822.6 17.0 %reshape.340 = bf16[2,2,1024,2048]{3,2,1,0:T(8,128)(2,1)} reshape(bf16[4,16,131072]{2,1,0:T(8,128)(2,1)} %copy.48) | data formatting | bytes 33554432 | tf_op jit(solution)/shard_map/reshape | solution.py:68
  842.6 86.0 %slice_reduce_fusion.3 = (bf16[16,131072]{1,0:T(8,128)(2,1)}, bf16[16,131072]{1,0:T(8,128)(2,1)}, bf16[16,131072]{1,0:T(8,128)(2,1)}, bf16[16,131072]{1,0:T(8,128)(2,1)}) fusion(bf16[4,16,131072]{2,0,1:T(4,128)(2,1)} %all-to-all-done.1), kind=kLoop, calls=%fused_computation.6 | loop fusion | bytes 33554432 | tf_op jit(solution)/shard_map/slice | solution.py:83
  928.7 4.8 squeeze.39
  933.5 4.8 squeeze.40
  938.3 4.9 squeeze.43
  943.2 4.8 squeeze.44
  948.0 1.8 slice_bitcast_fusion.2
  953.7 2.4 fusion.17
  957.1 2.4 fusion.14
  961.2 1.8 copy.51
  962.9 72.7 %all-to-all-start.2 = ((bf16[4,16,8192]{2,0,1:T(4,128)(2,1)}), bf16[4,16,8192]{2,0,1:T(4,128)(2,1)S(1)}, u32[]{:S(2)}, u32[]{:S(2)}) async-start(bf16[4,16,8192]{2,0,1:T(4,128)(2,1)} %copy.51), calls=%async_computation.2 | async-start | bytes 2097152 | tf_op jit(solution)/shard_map/all_to_all | solution.py:96
  1036.8 21.4 %all-to-all-done.2 = bf16[4,16,8192]{2,0,1:T(4,128)(2,1)S(1)} async-done(((bf16[4,16,8192]{2,0,1:T(4,128)(2,1)}), bf16[4,16,8192]{2,0,1:T(4,128)(2,1)S(1)}, u32[]{:S(2)}, u32[]{:S(2)}) %all-to-all-start.2) | async-done | bytes 1048608 | tf_op jit(solution)/shard_map/all_to_all | solution.py:96
  1058.9 2.8 dynamic-slice_bitcast_fusion
  1065.2 2.5 collective-permute-start.3
  1067.7 4.1 collective-permute-start.5
  1071.8 3.0 collective-permute-start.7
  1075.6 3.5 collective-permute-done.4
  1079.8 2.7 collective-permute-done.5
  1086.4 10.7 collective-permute-done.7
  1098.7 2.0 collective-permute-done.8
  1100.7 3.1 collective-permute-start.13
  1103.9 4.2 collective-permute-start.14
  1108.1 2.0 dynamic_update_slice.48
  1110.1 2.0 dynamic_update_slice.49
  1112.1 2.0 dynamic_update_slice.50
  1114.1 2.0 dynamic_update_slice.51
  1116.1 2.0 dynamic_update_slice.52
  1118.2 2.0 dynamic_update_slice.53
  1120.2 2.0 dynamic_update_slice.54
  1122.2 2.0 dynamic_update_slice.55
  1124.2 2.0 dynamic_update_slice.56
  1126.2 2.0 dynamic_update_slice.57
  1128.2 2.0 dynamic_update_slice.58
  1130.2 2.0 dynamic_update_slice.59
  1132.2 2.0 dynamic_update_slice.60
  1134.2 3.0 dynamic_update_slice.61
  1137.3 3.0 dynamic_update_slice.62
  1140.3 2.0 dynamic_update_slice.63
  (70 shorter events, 25.0 us)
Async XLA Ops:
  45.7 323.7 %all-to-all-start = ((bf16[4,16,131072]{2,0,1:T(4,128)(2,1)}), bf16[4,16,131072]{2,0,1:T(4,128)(2,1)}, u32[]{:S(2)}, u32[]{:S(2)}) async-start(bf16[4,16,131072]{2,0,1:T(4,128)(2,1)} %copy.46), calls=%async_computation | async-start | bytes 33554432 | tf_op jit(solution)/shard_map/all_to_all | solution.py:63
  418.0 73.9 %copy-start.5 = (s32[32]{0:T(128)S(1)}, s32[32]{0:T(128)}, u32[]{:S(2)}) copy-start(s32[32]{0:T(128)} %param.4) | copy-start | bytes 388
  418.0 73.9 %copy-start.6 = (s32[32]{0:T(128)S(1)}, s32[32]{0:T(128)}, u32[]{:S(2)}) copy-start(s32[32]{0:T(128)} %param.5) | copy-start | bytes 388
  418.0 385.9 %all-to-all-start.1 = ((bf16[4,16,131072]{2,0,1:T(4,128)(2,1)}), bf16[4,16,131072]{2,0,1:T(4,128)(2,1)}, u32[]{:S(2)}, u32[]{:S(2)}) async-start(bf16[4,16,131072]{2,0,1:T(4,128)(2,1)} %copy.47), calls=%async_computation.1 | async-start | bytes 33554432 | tf_op jit(solution)/shard_map/all_to_all | solution.py:67
  491.3 456.7 %all-gather.2.cloned.1.call-start = ((), (), s32[]{:S(2)}) async-start(), calls=%async_computation.3 | async-start | bytes 3145728 | tf_op jit(solution)/shard_map/all_gather | solution.py:79
  948.0 2.2 copy-start
  950.2 2.2 copy-start.4
  950.3 3.4 copy-start.2
  953.7 2.4 copy-start.1
  953.7 3.5 copy-start.3
  962.9 95.3 %all-to-all-start.2 = ((bf16[4,16,8192]{2,0,1:T(4,128)(2,1)}), bf16[4,16,8192]{2,0,1:T(4,128)(2,1)S(1)}, u32[]{:S(2)}, u32[]{:S(2)}) async-start(bf16[4,16,8192]{2,0,1:T(4,128)(2,1)} %copy.51), calls=%async_computation.2 | async-start | bytes 2097152 | tf_op jit(solution)/shard_map/all_to_all | solution.py:96
  1061.7 6.0 collective-permute-start
  1062.3 9.5 collective-permute-start.1
  1064.0 7.8 collective-permute-start.2
  1065.2 9.6 collective-permute-start.3
  1067.7 11.4 collective-permute-start.4
  1067.7 14.8 %collective-permute-start.5 = (bf16[4,1,8192]{2,1,0:T(2,128)(2,1)S(1)}, bf16[4,1,8192]{2,1,0:T(2,128)(2,1)S(1)}, u32[]{:S(2)}, u32[]{:S(2)}) collective-permute-start(bf16[4,1,8192]{2,1,0:T(2,128)(2,1)S(1)} %get-tuple-element.26), channel_id=1, source_target_pairs={{0,12},{2,14},{4,8},{6,10},{8,4},{10,6},{12,0},{14,2},{16,28},{18,... | collective-permute-start | bytes 196616 | tf_op jit(solution)/shard_map/ppermute | solution.py:112
  1071.8 13.0 %collective-permute-start.6 = (bf16[4,1,8192]{2,1,0:T(2,128)(2,1)S(1)}, bf16[4,1,8192]{2,1,0:T(2,128)(2,1)S(1)}, u32[]{:S(2)}, u32[]{:S(2)}) collective-permute-start(bf16[4,1,8192]{2,1,0:T(2,128)(2,1)S(1)} %get-tuple-element.25), channel_id=1, source_target_pairs={{0,14},{2,12},{4,10},{6,8},{8,6},{10,4},{12,2},{14,0},{16,30},{18,... | collective-permute-start | bytes 196616 | tf_op jit(solution)/shard_map/ppermute | solution.py:112
  1071.8 25.3 %collective-permute-start.7 = (bf16[4,1,8192]{2,1,0:T(2,128)(2,1)S(1)}, bf16[4,1,8192]{2,1,0:T(2,128)(2,1)S(1)}, u32[]{:S(2)}, u32[]{:S(2)}) collective-permute-start(bf16[4,1,8192]{2,1,0:T(2,128)(2,1)S(1)} %get-tuple-element.24), channel_id=1, source_target_pairs={{0,16},{2,18},{4,20},{6,22},{8,24},{10,26},{12,28},{14,30},{16,0},... | collective-permute-start | bytes 196616 | tf_op jit(solution)/shard_map/ppermute | solution.py:112
  1074.8 26.0 %collective-permute-start.8 = (bf16[4,1,8192]{2,1,0:T(2,128)(2,1)S(1)}, bf16[4,1,8192]{2,1,0:T(2,128)(2,1)S(1)}, u32[]{:S(2)}, u32[]{:S(2)}) collective-permute-start(bf16[4,1,8192]{2,1,0:T(2,128)(2,1)S(1)} %get-tuple-element.23), channel_id=1, source_target_pairs={{0,18},{2,16},{4,22},{6,20},{8,26},{10,24},{12,30},{14,28},{16,2},... | collective-permute-start | bytes 196616 | tf_op jit(solution)/shard_map/ppermute | solution.py:112
  1079.1 24.8 %collective-permute-start.9 = (bf16[4,1,8192]{2,1,0:T(2,128)(2,1)S(1)}, bf16[4,1,8192]{2,1,0:T(2,128)(2,1)S(1)}, u32[]{:S(2)}, u32[]{:S(2)}) collective-permute-start(bf16[4,1,8192]{2,1,0:T(2,128)(2,1)S(1)} %get-tuple-element.22), channel_id=1, source_target_pairs={{0,20},{2,22},{4,16},{6,18},{8,28},{10,30},{12,24},{14,26},{16,4},... | collective-permute-start | bytes 196616 | tf_op jit(solution)/shard_map/ppermute | solution.py:112
  1082.5 47.7 %collective-permute-start.10 = (bf16[4,1,8192]{2,1,0:T(2,128)(2,1)S(1)}, bf16[4,1,8192]{2,1,0:T(2,128)(2,1)S(1)}, u32[]{:S(2)}, u32[]{:S(2)}) collective-permute-start(bf16[4,1,8192]{2,1,0:T(2,128)(2,1)S(1)} %get-tuple-element.21), channel_id=1, source_target_pairs={{0,22},{2,20},{4,18},{6,16},{8,30},{10,28},{12,26},{14,24},{16,6},... | collective-permute-start | bytes 196616 | tf_op jit(solution)/shard_map/ppermute | solution.py:112
  1084.8 47.4 %collective-permute-start.11 = (bf16[4,1,8192]{2,1,0:T(2,128)(2,1)S(1)}, bf16[4,1,8192]{2,1,0:T(2,128)(2,1)S(1)}, u32[]{:S(2)}, u32[]{:S(2)}) collective-permute-start(bf16[4,1,8192]{2,1,0:T(2,128)(2,1)S(1)} %get-tuple-element.20), channel_id=1, source_target_pairs={{0,24},{2,26},{4,28},{6,30},{8,16},{10,18},{12,20},{14,22},{16,8},... | collective-permute-start | bytes 196616 | tf_op jit(solution)/shard_map/ppermute | solution.py:112
  1097.1 37.1 %collective-permute-start.12 = (bf16[4,1,8192]{2,1,0:T(2,128)(2,1)S(1)}, bf16[4,1,8192]{2,1,0:T(2,128)(2,1)}, u32[]{:S(2)}, u32[]{:S(2)}) collective-permute-start(bf16[4,1,8192]{2,1,0:T(2,128)(2,1)S(1)} %get-tuple-element.19), channel_id=1, source_target_pairs={{0,26},{2,24},{4,30},{6,28},{8,18},{10,16},{12,22},{14,20},{16,10}... | collective-permute-start | bytes 196616 | tf_op jit(solution)/shard_map/ppermute | solution.py:112
  1100.7 36.5 %collective-permute-start.13 = (bf16[4,1,8192]{2,1,0:T(2,128)(2,1)S(1)}, bf16[4,1,8192]{2,1,0:T(2,128)(2,1)}, u32[]{:S(2)}, u32[]{:S(2)}) collective-permute-start(bf16[4,1,8192]{2,1,0:T(2,128)(2,1)S(1)} %get-tuple-element.18), channel_id=1, source_target_pairs={{0,28},{2,30},{4,24},{6,26},{8,20},{10,22},{12,16},{14,18},{16,12}... | collective-permute-start | bytes 196616 | tf_op jit(solution)/shard_map/ppermute | solution.py:112
  1103.9 36.4 %collective-permute-start.14 = (bf16[4,1,8192]{2,1,0:T(2,128)(2,1)S(1)}, bf16[4,1,8192]{2,1,0:T(2,128)(2,1)S(1)}, u32[]{:S(2)}, u32[]{:S(2)}) collective-permute-start(bf16[4,1,8192]{2,1,0:T(2,128)(2,1)S(1)} %get-tuple-element.17), channel_id=1, source_target_pairs={{0,30},{2,28},{4,26},{6,24},{8,22},{10,20},{12,18},{14,16},{16,14}... | collective-permute-start | bytes 196616 | tf_op jit(solution)/shard_map/ppermute | solution.py:112
Sparse Core Ops, SparseCore 0:
  842.8 77.6 all-gather.1
